TPU v7x, 128 devices: a whole 4x4x4 slice. The times are simulated.
128 devices in a mesh: dp: 16 (over z, x_hi, core), mp: 8 (over y, x_lo).
Axes of the slice: x: 4 (x_hi: 2, x_lo: 2; x = x_hi * 2 + x_lo), y: 4, z: 4, core: 2. Of those that a mesh axis runs over, the one named last changes fastest.
Arguments:
- tokens: bfloat16 [16384, 1024], P(('dp', 'mp')), may hold values from -6 to 6
- cotangent: bfloat16 [16384, 1024], P(('dp', 'mp')), may hold values from -6 to 6
- lengths: int32 [16, 4], P('dp'), may hold values from 1 to 1021, as said below
- w_qkv: float32 [2, 1024, 3072], P(None, 'dp', 'mp'), may hold values from -0.1875 to 0.1875
- w_out: float32 [2, 1024, 1024], P(None, 'mp', 'dp'), may hold values from -0.75 to 0.75
- w_up: float32 [2, 1024, 4096], P(None, 'dp', 'mp'), may hold values from -0.1875 to 0.1875
- w_down: float32 [2, 4096, 1024], P(None, 'mp', 'dp'), may hold values from -0.09375 to 0.09375
- first_qkv: float32 [2, 1024, 3072], P(None, 'dp', 'mp'), may hold values from -80 to 80
- first_out: float32 [2, 1024, 1024], P(None, 'mp', 'dp'), may hold values from -24 to 24
- first_up: float32 [2, 1024, 4096], P(None, 'dp', 'mp'), may hold values from -24 to 24
- first_down: float32 [2, 4096, 1024], P(None, 'mp', 'dp'), may hold values from -48 to 48
- second_qkv: float32 [2, 1024, 3072], P(None, 'dp', 'mp'), may hold values from 425.984 to 6881.28
- second_out: float32 [2, 1024, 1024], P(None, 'mp', 'dp'), may hold values from 39.3216 to 622.592
- second_up: float32 [2, 1024, 4096], P(None, 'dp', 'mp'), may hold values from 39.3216 to 622.592
- second_down: float32 [2, 4096, 1024], P(None, 'mp', 'dp'), may hold values from 155.648 to 2457.6
- vectors: float32 [2, 12288], replicated, as said below
- vec_first: float32 [2, 12288], replicated, may hold values from -80 to 80
- vec_second: float32 [2, 12288], replicated, may hold values from 425.984 to 6881.28
Outputs:
- out_tokens: bfloat16 [16384, 1024], P(('dp', 'mp'))
- input_grad: float32 [16384, 1024], P(('dp', 'mp'))
- new_qkv: float32 [2, 1024, 3072], P(None, 'dp', 'mp')
- new_out: float32 [2, 1024, 1024], P(None, 'mp', 'dp')
- new_up: float32 [2, 1024, 4096], P(None, 'dp', 'mp')
- new_down: float32 [2, 4096, 1024], P(None, 'mp', 'dp')
- new_first_qkv: float32 [2, 1024, 3072], P(None, 'dp', 'mp')
- new_first_out: float32 [2, 1024, 1024], P(None, 'mp', 'dp')
- new_first_up: float32 [2, 1024, 4096], P(None, 'dp', 'mp')
- new_first_down: float32 [2, 4096, 1024], P(None, 'mp', 'dp')
- new_second_qkv: float32 [2, 1024, 3072], P(None, 'dp', 'mp')
- new_second_out: float32 [2, 1024, 1024], P(None, 'mp', 'dp')
- new_second_up: float32 [2, 1024, 4096], P(None, 'dp', 'mp')
- new_second_down: float32 [2, 4096, 1024], P(None, 'mp', 'dp')
- new_vectors: float32 [2, 12288], replicated
- new_vec_first: float32 [2, 12288], replicated
- new_vec_second: float32 [2, 12288], replicated
- bias_grads: float32 [2, 2, 1024], replicated
Inputs may be any that keep to these rules, and one draw needn't show every extreme that they name: Row g holds, in packing order, the lengths of the 4 sequences of data group g; a row sums to 1024; in every row one sequence begins within the group's first 128 tokens and ends within its last 128. `vectors`: gains about one, biases of both signs.
All inputs are finite; a program needn't handle non-finite values.
Results may differ from a plain program's by a relative error of at most 0.034.
Values may be sent and summed in bfloat16 or wider, within the bound.
No kernel may reach another device: no remote copies, remote signals or barrier semaphores. Data moves between devices by JAX's collectives and lax.ppermute only.
A program may use at most 128 MiB of HBM per device.

v0:
```python
import math

import jax
import jax.numpy as jnp
from jax import lax
from jax.sharding import PartitionSpec as P

D = 1024
HEADS = 16
HD = 64
FF = 4096
LAYERS = 2
STEP = 10


EPS_NORM = 1e-05
BETA_ONE = 0.9
BETA_TWO = 0.95
ADAM_EPS = 1e-08
RATE_MATRIX = 0.02
RATE_VECTOR = 0.4
DECAY_MATRIX = 0.1


def gelu_tanh(values):
    return jax.nn.gelu(values, approximate=True)


def layer_norm(source, gain, shift):
    row_mean = jnp.mean(source, -1, keepdims=True)
    centred = source - row_mean
    spread = jnp.mean(centred * centred, -1, keepdims=True)
    return centred * lax.rsqrt(spread + EPS_NORM) * gain + shift


def norm_back(source, gain, upstream, row_weight):
    row_mean = jnp.mean(source, -1, keepdims=True)
    centred = source - row_mean
    spread = jnp.mean(centred * centred, -1, keepdims=True)
    inv_std = lax.rsqrt(spread + EPS_NORM)
    unit = centred * inv_std
    scaled = upstream * gain
    d_source = inv_std * (
        scaled
        - jnp.mean(scaled, -1, keepdims=True)
        - unit * jnp.mean(scaled * unit, -1, keepdims=True)
    )
    counted = upstream * row_weight
    return (jnp.sum(counted * unit, 0), jnp.sum(counted, 0), d_source)


def adam_step(weight, first, second, grads, rate, decay):
    first_new = BETA_ONE * first + (1.0 - BETA_ONE) * grads
    second_new = BETA_TWO * second + (1.0 - BETA_TWO) * grads * grads
    first_hat = first_new / (1.0 - BETA_ONE**STEP)
    second_hat = second_new / (1.0 - BETA_TWO**STEP)
    weight_new = weight - rate * (first_hat / (jnp.sqrt(second_hat) + ADAM_EPS) + decay * weight)
    return (weight_new, first_new, second_new)


def contract_rows(left, right):
    return lax.dot_general(
        left, right, (((0,), (0,)), ((), ())), preferred_element_type=jnp.float32
    )


def contract_cols(left, right):
    return lax.dot_general(
        left, right, (((1,), (1,)), ((), ())), preferred_element_type=jnp.float32
    )


def local(
    tokens,
    cotangent,
    lengths,
    w_qkv,
    w_out,
    w_up,
    w_down,
    first_qkv,
    first_out,
    first_up,
    first_down,
    second_qkv,
    second_out,
    second_up,
    second_down,
    vectors,
    vec_first,
    vec_second,
):
    bf16 = jnp.bfloat16
    f32 = jnp.float32
    mp_index = lax.axis_index("mp")
    heads_dev = w_qkv.shape[2] // (3 * HD)
    hidden_dev = w_up.shape[2]
    rows_dev = tokens.shape[0]
    group_rows = rows_dev * lax.axis_size("mp")
    block_rows = min(512, group_rows)
    blocks = group_rows // block_rows
    score_scale = 1.0 / math.sqrt(HD)
    seq_ends = jnp.cumsum(lengths[0])
    positions = jnp.arange(group_rows, dtype=jnp.int32)
    segment = jnp.sum((positions[:, None] >= seq_ends[None, :]).astype(jnp.int32), axis=1)
    head_ids = mp_index * heads_dev + jnp.arange(heads_dev, dtype=jnp.int32)
    slopes = jnp.exp2(-8.0 * (head_ids.astype(f32) + 1.0) / HEADS)
    bias_start = 2 * D + mp_index * heads_dev * 2 * HD
    up_start = 7 * D + mp_index * hidden_dev

    def unpack(depth):
        row_params = vectors[depth]
        attn_bias = lax.dynamic_slice_in_dim(row_params, bias_start, heads_dev * 2 * HD, 0).reshape(
            heads_dev, 2, HD
        )
        up_bias = lax.dynamic_slice_in_dim(row_params, up_start, hidden_dev, 0)
        return (
            row_params[0:D],
            row_params[D : 2 * D],
            attn_bias,
            row_params[4 * D : 5 * D],
            row_params[5 * D : 6 * D],
            row_params[6 * D : 7 * D],
            up_bias,
            row_params[7 * D + FF : 8 * D + FF],
        )

    def low_weights(depth):
        return (
            w_qkv[depth].astype(bf16),
            w_out[depth].astype(bf16),
            w_up[depth].astype(bf16),
            w_down[depth].astype(bf16),
        )

    def gather_rows(values):
        return lax.all_gather(values, "mp", axis=0, tiled=True)

    def gather_grads(values):
        return lax.all_gather(values, "mp", axis=0, tiled=True)

    def sum_rows(left, right):

        def term(row_start, row_count):
            return jnp.dot(left, right, preferred_element_type=f32)

        return lax.psum_scatter(
            term(jnp.int32(0), lax.axis_size("mp") * rows_dev).astype(jnp.bfloat16),
            "mp",
            scatter_dimension=0,
            tiled=True,
        ).astype(jnp.float32)

    def sum_back(left, right):

        def term(row_start, row_count):
            return contract_cols(left, right)

        return lax.psum_scatter(
            term(jnp.int32(0), lax.axis_size("mp") * rows_dev).astype(jnp.bfloat16),
            "mp",
            scatter_dimension=0,
            tiled=True,
        ).astype(jnp.float32)

    def block_scores(query_blk, keys_all, first_row):
        raw_dot = jnp.einsum("qhd,khd->hqk", query_blk, keys_all, preferred_element_type=f32)
        query_pos = first_row + jnp.arange(block_rows, dtype=jnp.int32)
        distance = (query_pos[:, None] - positions[None, :]).astype(f32)
        scores = raw_dot * score_scale - slopes[:, None, None] * distance
        seg_query = lax.dynamic_slice_in_dim(segment, first_row, block_rows, 0)
        allowed = (seg_query[:, None] == segment[None, :]) & (
            positions[None, :] <= query_pos[:, None]
        )
        return (scores, allowed)

    def attend_back(queries, keys_all, values, log_total, d_context):

        def one_step(running, block):
            d_keys, d_values = running
            first_row = block * block_rows
            query_blk = lax.dynamic_slice_in_dim(queries, first_row, block_rows, 0)
            dctx_blk = lax.dynamic_slice_in_dim(d_context, first_row, block_rows, 0)
            scores, allowed = block_scores(query_blk, keys_all, first_row)
            attn_probs = jnp.where(
                allowed[None], jnp.exp(scores - log_total[block][..., None]), 0.0
            )
            d_prob = jnp.einsum("qhd,khd->hqk", dctx_blk, values, preferred_element_type=f32)
            inner_sum = jnp.sum(d_prob * attn_probs, -1, keepdims=True)
            dscore = (attn_probs * (d_prob - inner_sum)).astype(bf16)
            d_query = (
                jnp.einsum("hqk,khd->qhd", dscore, keys_all, preferred_element_type=f32)
                * score_scale
            )
            d_keys = (
                d_keys
                + jnp.einsum("hqk,qhd->khd", dscore, query_blk, preferred_element_type=f32)
                * score_scale
            )
            d_values = d_values + jnp.einsum(
                "hqk,qhd->khd", attn_probs.astype(bf16), dctx_blk, preferred_element_type=f32
            )
            return ((d_keys, d_values), d_query)

        blank_acc = jnp.zeros((group_rows, heads_dev, HD), f32)
        (d_keys, d_values), d_query = lax.scan(
            one_step, (blank_acc, blank_acc), jnp.arange(blocks, dtype=jnp.int32)
        )
        return (d_query.reshape(group_rows, heads_dev, HD), d_keys, d_values)

    residual = tokens.astype(f32)
    row_weight = jnp.ones((rows_dev, 1), f32)
    stored = []
    for depth in range(LAYERS):
        fetch_rounded_qkv, fetch_rounded_out, fetch_rounded_up, fetch_rounded_down = low_weights(
            depth
        )
        weights = (
            lax.all_gather(fetch_rounded_qkv, "dp", axis=0, tiled=True),
            lax.all_gather(fetch_rounded_out, "dp", axis=1, tiled=True),
            lax.all_gather(fetch_rounded_up, "dp", axis=0, tiled=True),
            lax.all_gather(fetch_rounded_down, "dp", axis=1, tiled=True),
        )
        mat_qkv, mat_out, mat_up, mat_down = weights
        gain_one, shift_one, attn_bias, out_bias, gain_two, shift_two, up_bias, down_bias = unpack(
            depth
        )
        normed = gather_rows(layer_norm(residual, gain_one, shift_one).astype(bf16))
        blank = jnp.zeros((heads_dev, HD), f32)
        proj_bias = jnp.stack([attn_bias[:, 0], blank, attn_bias[:, 1]], axis=1).reshape(-1)
        projected = (jnp.dot(normed, mat_qkv, preferred_element_type=f32) + proj_bias).astype(bf16)
        projected = projected.reshape(group_rows, heads_dev, 3, HD)
        attend_queries = projected[:, :, 0]
        attend_keys_all = projected[:, :, 1]
        attend_values = projected[:, :, 2]

        def one_block(block):
            first_row = block * block_rows
            query_blk = lax.dynamic_slice_in_dim(attend_queries, first_row, block_rows, 0)
            scores, allowed = block_scores(query_blk, attend_keys_all, first_row)
            scores = jnp.where(allowed[None], scores, -1e30)
            row_max = jnp.max(scores, -1, keepdims=True)
            powers = jnp.exp(scores - row_max)
            row_total = jnp.sum(powers, -1, keepdims=True)
            attn_probs = (powers / row_total).astype(bf16)
            context = jnp.einsum(
                "hqk,khd->qhd", attn_probs, attend_values, preferred_element_type=f32
            )
            return (context.astype(bf16), (row_max + jnp.log(row_total))[..., 0])

        context, attend_log_total = lax.map(one_block, jnp.arange(blocks, dtype=jnp.int32))
        context, log_total = (context.reshape(group_rows, heads_dev * HD), attend_log_total)
        hidden = residual + sum_rows(context, mat_out) + out_bias
        normed_two = gather_rows(layer_norm(hidden, gain_two, shift_two).astype(bf16))
        pre_act = jnp.dot(normed_two, mat_up, preferred_element_type=f32) + up_bias
        activation = gelu_tanh(pre_act).astype(bf16)
        stored.append(
            (
                residual,
                hidden,
                projected,
                context,
                log_total,
                pre_act,
                activation,
                normed,
                normed_two,
                weights,
            )
        )
        residual = hidden + sum_rows(activation, mat_down) + down_bias
    out_tokens = residual.astype(bf16)
    grad_flow = cotangent.astype(f32)
    layer_grads = [None] * LAYERS
    vector_rows = [None] * LAYERS
    for depth in reversed(range(LAYERS)):
        (
            residual,
            hidden,
            projected,
            context,
            log_total,
            pre_act,
            activation,
            normed,
            normed_two,
            weights,
        ) = stored[depth]
        gain_one, shift_one, attn_bias, out_bias, gain_two, shift_two, up_bias, down_bias = unpack(
            depth
        )
        rounded_qkv, rounded_out, rounded_up, rounded_down = low_weights(depth)
        mat_qkv, mat_out, mat_up, mat_down = (
            lax.all_gather(rounded_qkv, "dp", axis=0, tiled=True),
            lax.all_gather(rounded_out, "dp", axis=1, tiled=True),
            lax.all_gather(rounded_up, "dp", axis=0, tiled=True),
            lax.all_gather(rounded_down, "dp", axis=1, tiled=True),
        )
        normed = gather_rows(layer_norm(residual, gain_one, shift_one).astype(bf16))
        normed_two = gather_rows(layer_norm(hidden, gain_two, shift_two).astype(bf16))
        mlp_grad = grad_flow.astype(bf16)
        d_down_bias = jnp.sum(mlp_grad.astype(f32) * row_weight, 0)
        d_mlp = gather_grads(mlp_grad)
        g_down = contract_rows(activation, d_mlp)
        d_activation = contract_cols(d_mlp, mat_down)
        d_pre = jax.vjp(gelu_tanh, pre_act)[1](d_activation)[0].astype(bf16)
        d_up_bias = jnp.sum(d_pre.astype(f32), 0)
        g_up = contract_rows(normed_two, d_pre)
        d_normed_two = sum_back(d_pre, mat_up)
        d_gain_two, d_shift_two, d_hidden = norm_back(hidden, gain_two, d_normed_two, row_weight)
        grad_hidden = grad_flow + d_hidden
        branch_grad = grad_hidden.astype(bf16)
        d_out_bias = jnp.sum(branch_grad.astype(f32) * row_weight, 0)
        d_branch = gather_grads(branch_grad)
        g_out = contract_rows(context, d_branch)
        d_context = contract_cols(d_branch, mat_out).astype(bf16).reshape(group_rows, heads_dev, HD)
        d_query, d_keys, d_values = attend_back(
            projected[:, :, 0], projected[:, :, 1], projected[:, :, 2], log_total, d_context
        )
        d_projected = jnp.stack([d_query, d_keys, d_values], axis=2).astype(bf16)
        bias_sums = jnp.sum(d_projected.astype(f32), 0)
        d_attn_bias = jnp.stack([bias_sums[:, 0], bias_sums[:, 2]], axis=1).reshape(-1)
        d_projected = d_projected.reshape(group_rows, 3 * heads_dev * HD)
        g_qkv = contract_rows(normed, d_projected)
        d_normed = sum_back(d_projected, mat_qkv)
        d_gain_one, d_shift_one, d_residual = norm_back(residual, gain_one, d_normed, row_weight)
        grad_flow = grad_hidden + d_residual
        row_grad = jnp.concatenate(
            [
                d_gain_one,
                d_shift_one,
                jnp.zeros((2 * D,), f32),
                d_out_bias,
                d_gain_two,
                d_shift_two,
                jnp.zeros((FF,), f32),
                d_down_bias,
            ]
        )
        row_grad = lax.dynamic_update_slice_in_dim(row_grad, d_attn_bias, bias_start, 0)
        row_grad = lax.dynamic_update_slice_in_dim(row_grad, d_up_bias, up_start, 0)
        vector_rows[depth] = row_grad
        layer_grads[depth] = (
            lax.psum_scatter(
                g_qkv.astype(jnp.bfloat16), "dp", scatter_dimension=0, tiled=True
            ).astype(jnp.float32),
            lax.psum_scatter(
                g_out.astype(jnp.bfloat16), "dp", scatter_dimension=1, tiled=True
            ).astype(jnp.float32),
            lax.psum_scatter(
                g_up.astype(jnp.bfloat16), "dp", scatter_dimension=0, tiled=True
            ).astype(jnp.float32),
            lax.psum_scatter(
                g_down.astype(jnp.bfloat16), "dp", scatter_dimension=1, tiled=True
            ).astype(jnp.float32),
        )
    owned = tuple(
        (jnp.stack([layer_grads[depth][kind] for depth in range(LAYERS)]) for kind in range(4))
    )
    vector_grad = lax.psum(jnp.stack(vector_rows), ("dp", "mp"))
    out_rate = 0.8 / math.sqrt(D // 16)
    new_qkv, new_first_qkv, new_second_qkv = adam_step(
        w_qkv, first_qkv, second_qkv, owned[0], RATE_MATRIX, DECAY_MATRIX
    )
    new_out, new_first_out, new_second_out = adam_step(
        w_out, first_out, second_out, owned[1], out_rate, DECAY_MATRIX
    )
    new_up, new_first_up, new_second_up = adam_step(
        w_up, first_up, second_up, owned[2], RATE_MATRIX, DECAY_MATRIX
    )
    new_down, new_first_down, new_second_down = adam_step(
        w_down, first_down, second_down, owned[3], RATE_MATRIX, DECAY_MATRIX
    )
    new_vectors, new_vec_first, new_vec_second = adam_step(
        vectors, vec_first, vec_second, vector_grad, RATE_VECTOR, 0.0
    )
    bias_grads = jnp.stack(
        [vector_grad[:, 4 * D : 5 * D], vector_grad[:, 7 * D + FF : 8 * D + FF]], axis=1
    )
    return (
        out_tokens,
        grad_flow,
        new_qkv,
        new_out,
        new_up,
        new_down,
        new_first_qkv,
        new_first_out,
        new_first_up,
        new_first_down,
        new_second_qkv,
        new_second_out,
        new_second_up,
        new_second_down,
        new_vectors,
        new_vec_first,
        new_vec_second,
        bias_grads,
    )


def solution(mesh):
    placed = (
        P(("dp", "mp"), None),
        P(("dp", "mp"), None),
        P("dp", None),
        P(None, "dp", "mp"),
        P(None, "mp", "dp"),
        P(None, "dp", "mp"),
        P(None, "mp", "dp"),
        P(None, "dp", "mp"),
        P(None, "mp", "dp"),
        P(None, "dp", "mp"),
        P(None, "mp", "dp"),
        P(None, "dp", "mp"),
        P(None, "mp", "dp"),
        P(None, "dp", "mp"),
        P(None, "mp", "dp"),
        P(),
        P(),
        P(),
    )
    return jax.shard_map(
        local,
        mesh=mesh,
        in_specs=placed,
        out_specs=(
            P(("dp", "mp"), None),
            P(("dp", "mp"), None),
            P(None, "dp", "mp"),
            P(None, "mp", "dp"),
            P(None, "dp", "mp"),
            P(None, "mp", "dp"),
            P(None, "dp", "mp"),
            P(None, "mp", "dp"),
            P(None, "dp", "mp"),
            P(None, "mp", "dp"),
            P(None, "dp", "mp"),
            P(None, "mp", "dp"),
            P(None, "dp", "mp"),
            P(None, "mp", "dp"),
            P(),
            P(),
            P(),
            P(),
        ),
        check_vma=False,
    )
```

profile of v0, /device:TPU:0, one launch (start us, length us, event | category | flops | bytes accessed | tf_op | source)
XLA Modules:
  0.0 1788.5 jit_solution(4239082113580745797)
XLA Ops:
  98.3 54.2 %reduce-scatter.17.cloned.1.call-done = bf16[128,1024]{1,0:T(8,128)(2,1)} async-done(((bf16[1024,1024]{1,0:T(8,128)(2,1)}), bf16[128,1024]{1,0:T(8,128)(2,1)}) %reduce-scatter.17.cloned.1.call-update) | async-done | bytes 262160 | tf_op jit(solution)/shard_map/reduce_scatter | solution.py:147
  157.5 50.7 %all-gather.23.cloned.1.call-done = bf16[1024,1024]{1,0:T(8,128)(2,1)} async-done(((bf16[128,1024]{1,0:T(8,128)(2,1)}), bf16[1024,1024]{1,0:T(8,128)(2,1)}) %all-gather.23.cloned.1.call-update) | async-done | bytes 2097168 | tf_op jit(solution)/shard_map/all_gather | solution.py:137
  212.6 42.6 %all-gather.39.cloned.1.call-done = bf16[1,512,1024]{1,2,0:T(8,128)(2,1)} async-done(((bf16[1,512,64]{1,2,0:T(8,128)(2,1)}), bf16[1,512,1024]{1,2,0:T(8,128)(2,1)}) %all-gather.39.cloned.1.call-update) | async-done | bytes 1048592 | tf_op jit(solution)/shard_map/all_gather | solution.py:222
  259.9 51.3 %reduce-scatter.19.cloned.1.call-done = bf16[128,1024]{1,0:T(8,128)(2,1)} async-done(((bf16[1024,1024]{1,0:T(8,128)(2,1)}), bf16[128,1024]{1,0:T(8,128)(2,1)}) %reduce-scatter.19.cloned.1.call-update) | async-done | bytes 262160 | tf_op jit(solution)/shard_map/reduce_scatter | solution.py:147
  393.8 54.4 %reduce-scatter.21.cloned.1.call-done = bf16[128,1024]{1,0:T(8,128)(2,1)} async-done(((bf16[1024,1024]{1,0:T(8,128)(2,1)}), bf16[128,1024]{1,0:T(8,128)(2,1)}) %reduce-scatter.21.cloned.1.call-update) | async-done | bytes 262160 | tf_op jit(solution)/shard_map/reduce_scatter | solution.py:147
  451.7 50.3 %all-gather.27.cloned.1.call-done = bf16[1024,1024]{1,0:T(8,128)(2,1)} async-done(((bf16[128,1024]{1,0:T(8,128)(2,1)}), bf16[1024,1024]{1,0:T(8,128)(2,1)}) %all-gather.27.cloned.1.call-update) | async-done | bytes 2097168 | tf_op jit(solution)/shard_map/all_gather | solution.py:137
  506.4 42.6 %all-gather.43.cloned.1.call-done = bf16[1,512,1024]{1,2,0:T(8,128)(2,1)} async-done(((bf16[1,512,64]{1,2,0:T(8,128)(2,1)}), bf16[1,512,1024]{1,2,0:T(8,128)(2,1)}) %all-gather.43.cloned.1.call-update) | async-done | bytes 1048592 | tf_op jit(solution)/shard_map/all_gather | solution.py:222
  549.1 52.5 %all-gather.29.cloned.1.call-done = bf16[1024,1024]{1,0:T(8,128)(2,1)} async-done(((bf16[128,1024]{1,0:T(8,128)(2,1)}), bf16[1024,1024]{1,0:T(8,128)(2,1)}) %all-gather.29.cloned.1.call-update) | async-done | bytes 2097168 | tf_op jit(solution)/shard_map/all_gather | solution.py:140
  615.9 46.8 %reduce-scatter.25.cloned.1.call-done = bf16[128,1024]{1,0:T(8,128)(2,1)} async-done(((bf16[1024,1024]{1,0:T(8,128)(2,1)}), bf16[128,1024]{1,0:T(8,128)(2,1)}) %reduce-scatter.25.cloned.1.call-update) | async-done | bytes 262160 | tf_op jit(solution)/shard_map/reduce_scatter | solution.py:159
  664.5 52.2 %reduce-scatter.23.cloned.1.call-done = bf16[128,1024]{1,0:T(8,128)(2,1)} async-done(((bf16[1024,1024]{1,0:T(8,128)(2,1)}), bf16[128,1024]{1,0:T(8,128)(2,1)}) %reduce-scatter.23.cloned.1.call-update) | async-done | bytes 262160 | tf_op jit(solution)/shard_map/reduce_scatter | solution.py:147
  719.7 51.5 %all-gather.31.cloned.1.call-done = bf16[1024,1024]{1,0:T(8,128)(2,1)} async-done(((bf16[128,1024]{1,0:T(8,128)(2,1)}), bf16[1024,1024]{1,0:T(8,128)(2,1)}) %all-gather.31.cloned.1.call-update) | async-done | bytes 2097168 | tf_op jit(solution)/shard_map/all_gather | solution.py:140
  808.6 51.7 %reduce-scatter.27.cloned.1.call-done = bf16[128,1024]{1,0:T(8,128)(2,1)} async-done(((bf16[1024,1024]{1,0:T(8,128)(2,1)}), bf16[128,1024]{1,0:T(8,128)(2,1)}) %reduce-scatter.27.cloned.1.call-update) | async-done | bytes 262160 | tf_op jit(solution)/shard_map/reduce_scatter | solution.py:159
  863.8 51.3 %all-gather.33.cloned.1.call-done = bf16[1024,1024]{1,0:T(8,128)(2,1)} async-done(((bf16[128,1024]{1,0:T(8,128)(2,1)}), bf16[1024,1024]{1,0:T(8,128)(2,1)}) %all-gather.33.cloned.1.call-update) | async-done | bytes 2097168 | tf_op jit(solution)/shard_map/all_gather | solution.py:140
  923.8 51.7 %reduce-scatter.29.cloned.1.call-done = bf16[128,1024]{1,0:T(8,128)(2,1)} async-done(((bf16[1024,1024]{1,0:T(8,128)(2,1)}), bf16[128,1024]{1,0:T(8,128)(2,1)}) %reduce-scatter.29.cloned.1.call-update) | async-done | bytes 262160 | tf_op jit(solution)/shard_map/reduce_scatter | solution.py:159
  998.5 32.1 %all-gather.35.cloned.1.call-done = bf16[1024,1024]{1,0:T(8,128)(2,1)} async-done(((bf16[128,1024]{1,0:T(8,128)(2,1)}), bf16[1024,1024]{1,0:T(8,128)(2,1)}) %all-gather.35.cloned.1.call-update) | async-done | bytes 2097168 | tf_op jit(solution)/shard_map/all_gather | solution.py:140
  1100.5 70.1 %reduce-scatter.45.cloned.1.call-done = bf16[512,64]{0,1:T(8,128)(2,1)} async-done(((bf16[512,1024]{0,1:T(8,128)(2,1)}), bf16[512,64]{0,1:T(8,128)(2,1)}) %reduce-scatter.45.cloned.1.call-update) | async-done | bytes 65552 | tf_op jit(solution)/shard_map/reduce_scatter | solution.py:353
  1172.5 67.9 %reduce-scatter.43.cloned.1.call-done = bf16[64,512]{1,0:T(8,128)(2,1)} async-done(((bf16[1024,512]{1,0:T(8,128)(2,1)}), bf16[64,512]{1,0:T(8,128)(2,1)}) %reduce-scatter.43.cloned.1.call-update) | async-done | bytes 65552 | tf_op jit(solution)/shard_map/reduce_scatter | solution.py:350
  1240.4 70.2 %reduce-scatter.41.cloned.1.call-done = bf16[64,512]{1,0:T(8,128)(2,1)} async-done(((bf16[1024,512]{1,0:T(8,128)(2,1)}), bf16[64,512]{1,0:T(8,128)(2,1)}) %reduce-scatter.41.cloned.1.call-update) | async-done | bytes 65552 | tf_op jit(solution)/shard_map/reduce_scatter | solution.py:350
  1312.6 65.8 %reduce-scatter.39.cloned.1.call-done = bf16[128,64]{0,1:T(8,128)(2,1)} async-done(((bf16[128,1024]{0,1:T(8,128)(2,1)}), bf16[128,64]{0,1:T(8,128)(2,1)}) %reduce-scatter.39.cloned.1.call-update) | async-done | bytes 16400 | tf_op jit(solution)/shard_map/reduce_scatter | solution.py:347
  1378.4 67.9 %reduce-scatter.37.cloned.1.call-done = bf16[128,64]{0,1:T(8,128)(2,1)} async-done(((bf16[128,1024]{0,1:T(8,128)(2,1)}), bf16[128,64]{0,1:T(8,128)(2,1)}) %reduce-scatter.37.cloned.1.call-update) | async-done | bytes 16400 | tf_op jit(solution)/shard_map/reduce_scatter | solution.py:347
  1447.9 67.5 %reduce-scatter.35.cloned.1.call-done = bf16[64,384]{1,0:T(8,128)(2,1)} async-done(((bf16[1024,384]{1,0:T(8,128)(2,1)}), bf16[64,384]{1,0:T(8,128)(2,1)}) %reduce-scatter.35.cloned.1.call-update) | async-done | bytes 49168 | tf_op jit(solution)/shard_map/reduce_scatter | solution.py:344
  1515.4 69.3 %reduce-scatter.33.cloned.1.call-done = bf16[64,384]{1,0:T(8,128)(2,1)} async-done(((bf16[1024,384]{1,0:T(8,128)(2,1)}), bf16[64,384]{1,0:T(8,128)(2,1)}) %reduce-scatter.33.cloned.1.call-update) | async-done | bytes 49168 | tf_op jit(solution)/shard_map/reduce_scatter | solution.py:344
  1586.5 52.2 %reduce-scatter.31.cloned.1.call-done = bf16[128,1024]{1,0:T(8,128)(2,1)} async-done(((bf16[1024,1024]{1,0:T(8,128)(2,1)}), bf16[128,1024]{1,0:T(8,128)(2,1)}) %reduce-scatter.31.cloned.1.call-update) | async-done | bytes 262160 | tf_op jit(solution)/shard_map/reduce_scatter | solution.py:159
  1642.8 134.8 %all-reduce.2.cloned.1.call-done = f32[2,12288]{1,0:T(2,128)} async-done(((f32[2,12288]{1,0:T(2,128)}), f32[2,12288]{1,0:T(2,128)}) %all-reduce.2.cloned.1.call-update) | async-done | bytes 98320 | tf_op jit(solution)/shard_map/psum | solution.py:360
  (453 shorter events, 436.8 us)
Async XLA Ops:
  13.2 139.2 %reduce-scatter.17.cloned.1.call-start = ((), (), s32[]{:S(2)}) async-start(), calls=%async_computation.17 | async-start | bytes 2359296 | tf_op jit(solution)/shard_map/reduce_scatter | solution.py:147
  98.2 109.9 %all-gather.23.cloned.1.call-start = ((), (), s32[]{:S(2)}) async-start(), calls=%async_computation.18 | async-start | bytes 2359296 | tf_op jit(solution)/shard_map/all_gather | solution.py:137
  157.4 153.8 %reduce-scatter.19.cloned.1.call-start = ((), (), s32[]{:S(2)}) async-start(), calls=%async_computation.19 | async-start | bytes 2359296 | tf_op jit(solution)/shard_map/reduce_scatter | solution.py:147
  259.9 113.5 %all-gather.25.cloned.1.call-start = ((), (), s32[]{:S(2)}) async-start(), calls=%async_computation.20 | async-start | bytes 2359296 | tf_op jit(solution)/shard_map/all_gather | solution.py:137
  313.5 134.7 %reduce-scatter.21.cloned.1.call-start = ((), (), s32[]{:S(2)}) async-start(), calls=%async_computation.21 | async-start | bytes 2359296 | tf_op jit(solution)/shard_map/reduce_scatter | solution.py:147
  393.8 108.3 %all-gather.27.cloned.1.call-start = ((), (), s32[]{:S(2)}) async-start(), calls=%async_computation.22 | async-start | bytes 2359296 | tf_op jit(solution)/shard_map/all_gather | solution.py:137
  451.0 150.5 %all-gather.29.cloned.1.call-start = ((), (), s32[]{:S(2)}) async-start(), calls=%async_computation.24 | async-start | bytes 2359296 | tf_op jit(solution)/shard_map/all_gather | solution.py:140
  451.6 211.0 %reduce-scatter.25.cloned.1.call-start = ((), (), s32[]{:S(2)}) async-start(), calls=%async_computation.25 | async-start | bytes 2359296 | tf_op jit(solution)/shard_map/reduce_scatter | solution.py:159
  610.9 105.8 %reduce-scatter.23.cloned.1.call-start = ((), (), s32[]{:S(2)}) async-start(), calls=%async_computation.23 | async-start | bytes 2359296 | tf_op jit(solution)/shard_map/reduce_scatter | solution.py:147
  615.7 155.5 %all-gather.31.cloned.1.call-start = ((), (), s32[]{:S(2)}) async-start(), calls=%async_computation.26 | async-start | bytes 2359296 | tf_op jit(solution)/shard_map/all_gather | solution.py:140
  719.6 140.7 %reduce-scatter.27.cloned.1.call-start = ((), (), s32[]{:S(2)}) async-start(), calls=%async_computation.27 | async-start | bytes 2359296 | tf_op jit(solution)/shard_map/reduce_scatter | solution.py:159
  808.6 106.5 %all-gather.33.cloned.1.call-start = ((), (), s32[]{:S(2)}) async-start(), calls=%async_computation.28 | async-start | bytes 2359296 | tf_op jit(solution)/shard_map/all_gather | solution.py:140
  863.5 112.0 %reduce-scatter.29.cloned.1.call-start = ((), (), s32[]{:S(2)}) async-start(), calls=%async_computation.29 | async-start | bytes 2359296 | tf_op jit(solution)/shard_map/reduce_scatter | solution.py:159
  923.8 106.8 %all-gather.35.cloned.1.call-start = ((), (), s32[]{:S(2)}) async-start(), calls=%async_computation.30 | async-start | bytes 2359296 | tf_op jit(solution)/shard_map/all_gather | solution.py:140
  979.0 121.5 %reduce-scatter.47.cloned.1.call-start = ((), (), s32[]{:S(2)}) async-start(), calls=%async_computation.39 | async-start | bytes 1114112 | tf_op jit(solution)/shard_map/reduce_scatter | solution.py:353
  983.8 186.8 %reduce-scatter.45.cloned.1.call-start = ((), (), s32[]{:S(2)}) async-start(), calls=%async_computation.38 | async-start | bytes 1114112 | tf_op jit(solution)/shard_map/reduce_scatter | solution.py:353
  988.7 251.7 %reduce-scatter.43.cloned.1.call-start = ((), (), s32[]{:S(2)}) async-start(), calls=%async_computation.37 | async-start | bytes 1114112 | tf_op jit(solution)/shard_map/reduce_scatter | solution.py:350
  992.3 318.3 %reduce-scatter.41.cloned.1.call-start = ((), (), s32[]{:S(2)}) async-start(), calls=%async_computation.36 | async-start | bytes 1114112 | tf_op jit(solution)/shard_map/reduce_scatter | solution.py:350
  996.7 381.7 %reduce-scatter.39.cloned.1.call-start = ((), (), s32[]{:S(2)}) async-start(), calls=%async_computation.35 | async-start | bytes 278528 | tf_op jit(solution)/shard_map/reduce_scatter | solution.py:347
  998.4 447.9 %reduce-scatter.37.cloned.1.call-start = ((), (), s32[]{:S(2)}) async-start(), calls=%async_computation.34 | async-start | bytes 278528 | tf_op jit(solution)/shard_map/reduce_scatter | solution.py:347
  1033.9 481.6 %reduce-scatter.35.cloned.1.call-start = ((), (), s32[]{:S(2)}) async-start(), calls=%async_computation.33 | async-start | bytes 835584 | tf_op jit(solution)/shard_map/reduce_scatter | solution.py:344
  1038.1 546.6 %reduce-scatter.33.cloned.1.call-start = ((), (), s32[]{:S(2)}) async-start(), calls=%async_computation.32 | async-start | bytes 835584 | tf_op jit(solution)/shard_map/reduce_scatter | solution.py:344
  1067.7 570.9 %reduce-scatter.31.cloned.1.call-start = ((), (), s32[]{:S(2)}) async-start(), calls=%async_computation.31 | async-start | bytes 2359296 | tf_op jit(solution)/shard_map/reduce_scatter | solution.py:159
  1070.6 707.0 %all-reduce.2.cloned.1.call-start = ((), (), s32[]{:S(2)}) async-start(), calls=%async_computation.40 | async-start | bytes 196608 | tf_op jit(solution)/shard_map/psum | solution.py:360
  (73 other events, 8269.3 us)
Sparse Core Ops, SparseCore 0:
  13.3 64.0 all-gather.20
  97.5 54.8 reduce-scatter.16
  313.6 59.7 all-gather.24
  393.1 55.0 reduce-scatter.20
  611.0 51.5 reduce-scatter.24
  664.9 51.7 reduce-scatter.22
  808.7 51.5 reduce-scatter.26
  923.9 51.5 reduce-scatter.28
  1640.9 136.6 all-reduce.1
Sparse Core Ops, SparseCore 1:
  100.9 48.0 all-gather.36
  156.7 51.4 all-gather.22
  211.1 44.1 all-gather.38
  259.9 51.2 reduce-scatter.18
  396.8 48.0 all-gather.40
  450.5 51.4 all-gather.26
  504.9 44.1 all-gather.42
  550.6 50.9 all-gather.28
  719.7 51.4 all-gather.30
  863.6 51.4 all-gather.32
  979.1 51.4 all-gather.34
  1034.4 66.1 reduce-scatter.46
  1104.7 65.9 reduce-scatter.44
  1174.4 65.9 reduce-scatter.42
  1244.6 65.9 reduce-scatter.40
  1314.2 64.1 reduce-scatter.38
  1382.1 64.2 reduce-scatter.36
  1450.2 65.2 reduce-scatter.34
  1519.6 65.1 reduce-scatter.32
  1587.2 51.4 reduce-scatter.30
where the time goes:
time: 1800 us; the launch traced here: 1790 us
  waiting for transfers between devices  1440 us (80%)
  blocking collectives  116 us (6%)
  matrix products  113 us (6%)
  other arithmetic  54.9 us (3%)
  local copies, waits for them, and re-layouts  35.1 us (2%)
    reduce_scatter x4, waiting for transfers between devices, sum_rows(): lax.psum_scatter(term(jnp.int32(0), lax.axis_size('mp') * rows_dev).astyp...  212 us
    reduce_scatter x4, waiting for transfers between devices, sum_back(): lax.psum_scatter(term(jnp.int32(0), lax.axis_size('mp') * rows_dev).astyp...  202 us
    all_gather x4, waiting for transfers between devices, gather_grads(): return lax.all_gather(values, 'mp', axis=0, tiled=True)  187 us
    reduce_scatter x2, waiting for transfers between devices, local(): lax.psum_scatter(g_up.astype(jnp.bfloat16), 'dp', scatter_dimension=0, ti...  138 us
    reduce_scatter x2, waiting for transfers between devices, local(): lax.psum_scatter(g_qkv.astype(jnp.bfloat16), 'dp', scatter_dimension=0, t...  137 us
    psum x1, waiting for transfers between devices, local(): vector_grad = lax.psum(jnp.stack(vector_rows), ('dp', 'mp'))  135 us
    reduce_scatter x2, waiting for transfers between devices, local(): lax.psum_scatter(g_out.astype(jnp.bfloat16), 'dp', scatter_dimension=1, t...  134 us
    all_gather x4, waiting for transfers between devices, gather_rows(): return lax.all_gather(values, 'mp', axis=0, tiled=True)  105 us
  transfers between devices with their start and end apart: 29, of which 27 were waited for; matrix products, arithmetic and copies ran while one was open for 5% of the time, Pallas kernels for 0%

commit v1 on v0

v1 whole, which is shorter than its diff:
```python
import math

import jax
import jax.numpy as jnp
from jax import lax
from jax.experimental import pallas as pl
from jax.experimental.pallas import tpu as pltpu
from jax.sharding import PartitionSpec as P

D = 1024
HEADS = 16
HD = 64
FF = 4096
LAYERS = 2
STEP = 10


EPS_NORM = 1e-05
BETA_ONE = 0.9
BETA_TWO = 0.95
ADAM_EPS = 1e-08
RATE_MATRIX = 0.02
RATE_VECTOR = 0.4
DECAY_MATRIX = 0.1


def gelu_tanh(values):
    return jax.nn.gelu(values, approximate=True)


def layer_norm(source, gain, shift):
    row_mean = jnp.mean(source, -1, keepdims=True)
    centred = source - row_mean
    spread = jnp.mean(centred * centred, -1, keepdims=True)
    return centred * lax.rsqrt(spread + EPS_NORM) * gain + shift


def norm_back(source, gain, upstream, row_weight):
    row_mean = jnp.mean(source, -1, keepdims=True)
    centred = source - row_mean
    spread = jnp.mean(centred * centred, -1, keepdims=True)
    inv_std = lax.rsqrt(spread + EPS_NORM)
    unit = centred * inv_std
    scaled = upstream * gain
    d_source = inv_std * (
        scaled
        - jnp.mean(scaled, -1, keepdims=True)
        - unit * jnp.mean(scaled * unit, -1, keepdims=True)
    )
    counted = upstream * row_weight
    return (jnp.sum(counted * unit, 0), jnp.sum(counted, 0), d_source)


def adam_step(weight, first, second, grads, rate, decay):
    first_new = BETA_ONE * first + (1.0 - BETA_ONE) * grads
    second_new = BETA_TWO * second + (1.0 - BETA_TWO) * grads * grads
    first_hat = first_new / (1.0 - BETA_ONE**STEP)
    second_hat = second_new / (1.0 - BETA_TWO**STEP)
    weight_new = weight - rate * (first_hat / (jnp.sqrt(second_hat) + ADAM_EPS) + decay * weight)
    return (weight_new, first_new, second_new)


def contract_rows(left, right):
    return lax.dot_general(
        left, right, (((0,), (0,)), ((), ())), preferred_element_type=jnp.float32
    )


def contract_cols(left, right):
    return lax.dot_general(
        left, right, (((1,), (1,)), ((), ())), preferred_element_type=jnp.float32
    )


N_MP = 8
N_DP = 16
N_Y = 4
MP = "mp"
DP = "dp"
COLUMNS = [[0, 2, 4, 6], [1, 3, 5, 7]]
BLOCK = 64
SECTIONS = (0, 1, 4, 5, 6, 11)
CUT_DOWN = 1024
CUT_QKV = 2048
END_QKV = 2432


def pair_swap(values):
    return lax.ppermute(values, MP, [(i, i ^ 1) for i in range(N_MP)])


def exchange(pieces):
    return lax.all_to_all(pieces, MP, 0, 0)


def exchange_column(pieces):
    return lax.all_to_all(pieces, MP, 0, 0, axis_index_groups=COLUMNS)


def gather_group(values):
    copies = jnp.broadcast_to(values[None], (N_MP,) + values.shape)
    return exchange(copies).reshape(-1, values.shape[1])


def scatter_group(values):
    pieces = values.reshape(N_MP, -1, values.shape[1])
    return jnp.sum(exchange(pieces).astype(jnp.float32), axis=0)


def gather_column(values):
    copies = jnp.broadcast_to(values[None], (N_Y,) + values.shape)
    return exchange_column(copies).reshape(-1, values.shape[1])


def scatter_column(values):
    pieces = values.reshape(N_Y, -1, values.shape[1])
    return jnp.sum(exchange_column(pieces).astype(jnp.float32), axis=0)


def exchange_dp(pieces):
    return lax.all_to_all(pieces, DP, 0, 0)


def gather_dp_exchange(shard):
    copies = jnp.broadcast_to(shard[None], (N_DP,) + shard.shape)
    return exchange_dp(copies).reshape(-1, shard.shape[1])


def gather_dp(shard):
    return lax.all_gather(shard, DP, axis=0, tiled=True)


def scatter_dp(values):
    return lax.psum_scatter(values, DP, scatter_dimension=0, tiled=True)


def heads_from_rows(values):
    pieces = values.reshape(values.shape[0], N_MP, -1)
    return exchange(jnp.swapaxes(pieces, 0, 1)).reshape(-1, pieces.shape[2])


Q_ROWS = 256
ATTN_VMEM = 40 * 1024 * 1024


def nt_dot(left, right):
    return lax.dot_general(
        left, right, (((1,), (1,)), ((), ())), preferred_element_type=jnp.float32
    )


def tn_dot(left, right):
    return lax.dot_general(
        left, right, (((0,), (0,)), ((), ())), preferred_element_type=jnp.float32
    )


def head_part(joined_ref, head, part):
    first = (3 * head + part) * HD
    return joined_ref[:, first : first + HD]


def score_chunks(queries, keys_all, block, slope, places, starts, lowest):
    own = slice(block * Q_ROWS, (block + 1) * Q_ROWS)
    query_blk = queries[own]
    first_place = starts[:, own]
    chunks = []
    for part in range(block + 1):
        rows = slice(part * Q_ROWS, (part + 1) * Q_ROWS)
        place = places + float(part * Q_ROWS)
        score = nt_dot(keys_all[rows], query_blk) + place * slope
        allowed = place >= first_place
        if part == block:
            row_at = lax.broadcasted_iota(jnp.int32, (Q_ROWS, Q_ROWS), 0)
            lane_at = lax.broadcasted_iota(jnp.int32, (Q_ROWS, Q_ROWS), 1)
            allowed = allowed & (row_at <= lane_at)
        chunks.append(jnp.where(allowed, score, lowest))
    return chunks


def attend_kernel(slopes_ref, joined_ref, starts_ref, context_ref, log_ref):
    bf16 = jnp.bfloat16
    group_rows = joined_ref.shape[0]
    starts = starts_ref[...]
    places = lax.broadcasted_iota(jnp.int32, (Q_ROWS, Q_ROWS), 0).astype(jnp.float32)
    for head in range(2):
        queries = head_part(joined_ref, head, 0) * bf16(1.0 / math.sqrt(HD))
        keys_all = head_part(joined_ref, head, 1)
        values = head_part(joined_ref, head, 2)
        slope = slopes_ref[head]
        for block in range(group_rows // Q_ROWS):
            chunks = score_chunks(queries, keys_all, block, slope, places, starts, -1e30)
            top = jnp.max(chunks[0], axis=0, keepdims=True)
            for chunk in chunks[1:]:
                top = jnp.maximum(top, jnp.max(chunk, axis=0, keepdims=True))
            total = jnp.zeros_like(top)
            context = jnp.zeros((HD, Q_ROWS), jnp.float32)
            for part, chunk in enumerate(chunks):
                power = jnp.exp(chunk - top)
                total = total + jnp.sum(power, axis=0, keepdims=True)
                rows = slice(part * Q_ROWS, (part + 1) * Q_ROWS)
                context = context + tn_dot(values[rows], power.astype(bf16))
            context = (context / total).astype(bf16)
            for half in range(2):
                context_ref[2 * block + half, head * HD : (head + 1) * HD, :] = context[
                    :, half * 128 : (half + 1) * 128
                ]
            own = slice(block * Q_ROWS, (block + 1) * Q_ROWS)
            log_ref[head : head + 1, own] = top + jnp.log(total)


def attend_back_kernel(
    slopes_ref,
    joined_ref,
    d_context_ref,
    starts_ref,
    log_ref,
    d_joined_ref,
    sums_ref,
    d_keys_ref,
    d_values_ref,
):
    bf16 = jnp.bfloat16
    scale = 1.0 / math.sqrt(HD)
    group_rows = joined_ref.shape[0]
    starts = starts_ref[...]
    places = lax.broadcasted_iota(jnp.int32, (Q_ROWS, Q_ROWS), 0).astype(jnp.float32)
    for head in range(2):
        queries = head_part(joined_ref, head, 0) * bf16(scale)
        keys_all = head_part(joined_ref, head, 1)
        values = head_part(joined_ref, head, 2)
        d_context = d_context_ref[:, head * HD : (head + 1) * HD]
        slope = slopes_ref[head]
        for block in range(group_rows // Q_ROWS):
            own = slice(block * Q_ROWS, (block + 1) * Q_ROWS)
            chunks = score_chunks(queries, keys_all, block, slope, places, starts, -1e30)
            log_total = log_ref[head : head + 1, own]
            probs = []
            d_probs = []
            inner = jnp.zeros((1, Q_ROWS), jnp.float32)
            for part, chunk in enumerate(chunks):
                rows = slice(part * Q_ROWS, (part + 1) * Q_ROWS)
                prob = jnp.exp(chunk - log_total)
                d_prob = nt_dot(values[rows], d_context[own])
                inner = inner + jnp.sum(prob * d_prob, axis=0, keepdims=True)
                probs.append(prob)
                d_probs.append(d_prob)
            d_query = jnp.zeros((HD, Q_ROWS), jnp.float32)
            for part in range(block + 1):
                rows = slice(part * Q_ROWS, (part + 1) * Q_ROWS)
                d_score = (probs[part] * (d_probs[part] - inner)).astype(bf16)
                d_key = jnp.dot(d_score, queries[own], preferred_element_type=jnp.float32)
                d_value = jnp.dot(
                    probs[part].astype(bf16), d_context[own], preferred_element_type=jnp.float32
                )
                if part == block:
                    d_keys_ref[rows, :] = d_key
                    d_values_ref[rows, :] = d_value
                else:
                    d_keys_ref[rows, :] += d_key
                    d_values_ref[rows, :] += d_value
                d_query = d_query + tn_dot(keys_all[rows], d_score)
            first = 3 * head * HD
            d_joined_ref[own, first : first + HD] = (d_query * scale).T.astype(bf16)
        d_joined_ref[:, first + HD : first + 2 * HD] = d_keys_ref[...].astype(bf16)
        d_joined_ref[:, first + 2 * HD : first + 3 * HD] = d_values_ref[...].astype(bf16)
    sums_ref[...] = jnp.sum(d_joined_ref[...].astype(jnp.float32), axis=0, keepdims=True)


def attend(slopes, joined, starts):
    group_rows = joined.shape[0]
    in_vmem = pl.BlockSpec(memory_space=pltpu.VMEM)
    return pl.pallas_call(
        attend_kernel,
        out_shape=(
            jax.ShapeDtypeStruct((group_rows // 128, 2 * HD, 128), jnp.bfloat16),
            jax.ShapeDtypeStruct((2, group_rows), jnp.float32),
        ),
        in_specs=[pl.BlockSpec(memory_space=pltpu.SMEM), in_vmem, in_vmem],
        out_specs=(in_vmem, in_vmem),
        compiler_params=pltpu.CompilerParams(vmem_limit_bytes=ATTN_VMEM),
        cost_estimate=pl.CostEstimate(
            flops=8 * 2 * HD * group_rows * group_rows,
            bytes_accessed=2 * 512 * group_rows,
            transcendentals=2 * group_rows * group_rows,
        ),
    )(slopes, joined, starts)


def attend_back(slopes, joined, d_context, starts, log_total):
    group_rows = joined.shape[0]
    in_vmem = pl.BlockSpec(memory_space=pltpu.VMEM)
    return pl.pallas_call(
        attend_back_kernel,
        out_shape=(
            jax.ShapeDtypeStruct(joined.shape, jnp.bfloat16),
            jax.ShapeDtypeStruct((1, joined.shape[1]), jnp.float32),
        ),
        in_specs=[pl.BlockSpec(memory_space=pltpu.SMEM)] + [in_vmem] * 4,
        out_specs=(in_vmem, in_vmem),
        scratch_shapes=[pltpu.VMEM((group_rows, HD), jnp.float32)] * 2,
        compiler_params=pltpu.CompilerParams(vmem_limit_bytes=ATTN_VMEM),
        cost_estimate=pl.CostEstimate(
            flops=20 * 2 * HD * group_rows * group_rows,
            bytes_accessed=4 * 512 * group_rows,
            transcendentals=2 * group_rows * group_rows,
        ),
    )(slopes, joined, d_context, starts, log_total)


def gradient_kernel(
    normed_ref, d_pre_ref, d_mlp_ref, act_ref, d_branch_ref, context_ref, joined_ref, left_ref
):
    tile = 256

    def keep(first, result):
        joined_ref[:, first : first + tile] = result.astype(jnp.bfloat16)

    firsts = ((0, 256, 1024, 1280), (512, 768, 1536, 1792))
    for kind, (left, right) in enumerate(((normed_ref, d_pre_ref), (d_mlp_ref, act_ref))):
        left_ref[...] = left[...].T
        for step, first in enumerate(firsts[kind]):
            cols = slice(step * tile, (step + 1) * tile)
            keep(
                first,
                jnp.dot(left_ref[...], right[:, cols], preferred_element_type=jnp.float32),
            )
    branch = d_branch_ref[...].T
    for step in range(D // tile):
        rows = slice(step * tile, (step + 1) * tile)
        keep(2 * D + step * tile, nt_dot(branch, context_ref[rows, :]))


def gradients(normed_two, d_pre, d_mlp, activation, branch_grad, context):
    in_vmem = pl.BlockSpec(memory_space=pltpu.VMEM)
    rows = normed_two.shape[0]
    return pl.pallas_call(
        gradient_kernel,
        out_shape=jax.ShapeDtypeStruct((D, 3 * D), jnp.bfloat16),
        in_specs=[in_vmem] * 6,
        out_specs=in_vmem,
        scratch_shapes=[pltpu.VMEM((D, rows), jnp.bfloat16)],
        compiler_params=pltpu.CompilerParams(vmem_limit_bytes=ATTN_VMEM),
        cost_estimate=pl.CostEstimate(
            flops=2 * D * 2 * D * rows + 2 * D * D * branch_grad.shape[0],
            bytes_accessed=12 * 1024 * 1024,
            transcendentals=0,
        ),
    )(normed_two, d_pre, d_mlp, activation, branch_grad, context)


def local(
    tokens,
    cotangent,
    lengths,
    w_qkv,
    w_out,
    w_up,
    w_down,
    first_qkv,
    first_out,
    first_up,
    first_down,
    second_qkv,
    second_out,
    second_up,
    second_down,
    vectors,
    vec_first,
    vec_second,
):
    bf16 = jnp.bfloat16
    f32 = jnp.float32
    mp_index = lax.axis_index(MP)
    heads_dev = w_qkv.shape[2] // (3 * HD)
    hidden_dev = w_up.shape[2]
    rows_dev = tokens.shape[0]
    group_rows = rows_dev * N_MP
    seq_ends = jnp.cumsum(lengths[0])
    head_ids = mp_index * heads_dev + jnp.arange(heads_dev, dtype=jnp.int32)
    slopes = jnp.exp2(-8.0 * (head_ids.astype(f32) + 1.0) / HEADS)
    bias_start = 2 * D + mp_index * heads_dev * 2 * HD
    up_start = 7 * D + mp_index * hidden_dev

    other_up_start = 7 * D + jnp.bitwise_xor(mp_index, 1) * hidden_dev
    positions = jnp.arange(group_rows, dtype=jnp.int32)
    later = positions[:, None] >= seq_ends[None, :]
    starts = jnp.max(jnp.where(later, seq_ends[None, :], 0), axis=1).astype(f32)[None]

    def unpack(depth):
        row_params = vectors[depth]
        features = [row_params[f * D : (f + 1) * D] for f in SECTIONS]
        attn_bias = lax.dynamic_slice_in_dim(row_params, bias_start, heads_dev * 2 * HD, 0).reshape(
            heads_dev, 2, HD
        )
        up_bias = jnp.concatenate(
            [
                lax.dynamic_slice_in_dim(row_params, up_start, hidden_dev, 0),
                lax.dynamic_slice_in_dim(row_params, other_up_start, hidden_dev, 0),
            ]
        )
        return (
            features[0],
            features[1],
            attn_bias,
            features[2],
            features[3],
            features[4],
            up_bias,
            features[5],
        )

    def gather_weights():
        own_mlp = jnp.concatenate(
            [part for d in range(LAYERS) for part in (w_up[d], w_down[d].T)], axis=1
        ).astype(bf16)
        other_mlp = pair_swap(own_mlp)
        out_rows = exchange(
            jnp.broadcast_to(w_out.astype(bf16)[None], (N_MP,) + w_out.shape)
        )
        out_cols = jnp.transpose(out_rows, (3, 1, 0, 2)).reshape(-1, LAYERS, D)

        def mlp_parts(depth):
            base = 2 * depth * hidden_dev
            up_cols = slice(base, base + hidden_dev)
            down_cols = slice(base + hidden_dev, base + 2 * hidden_dev)
            return [
                own_mlp[:, up_cols],
                other_mlp[:, up_cols],
                own_mlp[:, down_cols],
                other_mlp[:, down_cols],
            ]

        first = gather_dp(jnp.concatenate(mlp_parts(0) + [w_qkv[0].astype(bf16)], axis=1))
        first_out = gather_dp_exchange(out_cols[:, 0])
        second = gather_dp(
            jnp.concatenate(
                mlp_parts(1) + [w_qkv[1].astype(bf16), out_cols[:, 1]],
                axis=1,
            )
        )
        return ((first, first_out), (second, second[:, END_QKV:]))

    residual = tokens.astype(f32)
    d_mlp = lax.all_gather(cotangent, MP, axis=0, tiled=True, axis_index_groups=COLUMNS)
    row_weight = jnp.ones((rows_dev, 1), f32)
    stored = []
    joined = gather_weights()
    for depth in range(LAYERS):
        weights, mat_out = joined[depth]
        mat_qkv = weights[:, CUT_QKV:END_QKV]
        gain_one, shift_one, attn_bias, out_bias, gain_two, shift_two, up_bias, down_bias = unpack(
            depth
        )
        normed = gather_group(layer_norm(residual, gain_one, shift_one).astype(bf16))
        blank = jnp.zeros((heads_dev, HD), f32)
        proj_bias = jnp.stack([attn_bias[:, 0], blank, attn_bias[:, 1]], axis=1).reshape(-1)
        projected = (
            jnp.dot(normed, mat_qkv, preferred_element_type=f32) + proj_bias
        ).astype(bf16)
        context, log_total = attend(slopes, projected, starts)
        context = exchange(context).reshape(D, rows_dev)
        branch = lax.dot_general(
            context, mat_out, (((0,), (1,)), ((), ())), preferred_element_type=f32
        )
        hidden = residual + branch + out_bias
        normed_two = gather_column(layer_norm(hidden, gain_two, shift_two).astype(bf16))
        pre_act = (
            jnp.dot(normed_two, weights[:, :CUT_DOWN], preferred_element_type=f32) + up_bias
        )
        activation = gelu_tanh(pre_act).astype(bf16)
        stored.append(
            (
                residual,
                hidden,
                projected,
                context,
                log_total,
                pre_act,
                activation,
                normed,
                normed_two,
            )
        )
        branch_two = contract_cols(activation, weights[:, CUT_DOWN:CUT_QKV]).astype(bf16)
        if depth < LAYERS - 1:
            residual = hidden + scatter_column(branch_two) + down_bias
        else:
            last_base = hidden + down_bias
    grad_flow = cotangent.astype(f32)
    layer_grads = [None] * LAYERS
    vector_rows = [None] * LAYERS
    held = [None] * LAYERS
    held_qkv = [None] * LAYERS
    for depth in reversed(range(LAYERS)):
        (
            residual,
            hidden,
            projected,
            context,
            log_total,
            pre_act,
            activation,
            normed,
            normed_two,
        ) = stored[depth]
        weights, mat_out = joined[depth]
        mat_qkv = weights[:, CUT_QKV:END_QKV]
        gain_one, shift_one, attn_bias, out_bias, gain_two, shift_two, up_bias, down_bias = unpack(
            depth
        )
        mlp_grad = grad_flow.astype(bf16)
        d_down_bias = jnp.sum(mlp_grad.astype(f32) * row_weight, 0)
        if depth < LAYERS - 1:
            d_mlp = gather_column(mlp_grad)
        d_activation = jnp.dot(d_mlp, weights[:, CUT_DOWN:CUT_QKV], preferred_element_type=f32)
        d_pre = jax.vjp(gelu_tanh, pre_act)[1](d_activation)[0].astype(bf16)
        if depth == LAYERS - 1:
            branch_two, d_pre = lax.optimization_barrier((branch_two, d_pre))
            last_branch = lax.psum_scatter(
                branch_two,
                MP,
                scatter_dimension=0,
                tiled=True,
                axis_index_groups=COLUMNS,
            )
        d_up_bias = jnp.sum(d_pre.astype(f32), 0)
        d_normed_two = scatter_column(contract_cols(d_pre, weights[:, :CUT_DOWN]).astype(bf16))
        d_gain_two, d_shift_two, d_hidden = norm_back(hidden, gain_two, d_normed_two, row_weight)
        grad_hidden = grad_flow + d_hidden
        branch_grad = grad_hidden.astype(bf16)
        d_out_bias = jnp.sum(branch_grad.astype(f32) * row_weight, 0)
        g_joined = gradients(normed_two, d_pre, d_mlp, activation, branch_grad, context)
        d_context = heads_from_rows(
            jnp.dot(branch_grad, mat_out, preferred_element_type=f32).astype(bf16)
        )
        g_joined, d_context = lax.optimization_barrier((g_joined, d_context))
        g_joined = scatter_dp(g_joined)
        d_projected, bias_sums = attend_back(slopes, projected, d_context, starts, log_total)
        bias_sums = bias_sums.reshape(heads_dev, 3, HD)
        d_attn_bias = jnp.stack([bias_sums[:, 0], bias_sums[:, 2]], axis=1).reshape(-1)
        if depth == 0:
            d_projected, held[1], last_branch = lax.optimization_barrier(
                (d_projected, held[1], last_branch)
            )
        d_normed = scatter_group(contract_cols(d_projected, mat_qkv).astype(bf16))
        g_qkv = contract_rows(normed, d_projected).astype(bf16)
        held[depth] = g_joined
        held_qkv[depth] = g_qkv
        d_gain_one, d_shift_one, d_residual = norm_back(residual, gain_one, d_normed, row_weight)
        grad_flow = grad_hidden + d_residual
        blank = jnp.zeros((FF,), f32)
        row_grad = jnp.concatenate(
            [
                d_gain_one,
                d_shift_one,
                blank[: 2 * D],
                d_out_bias,
                d_gain_two,
                d_shift_two,
                blank,
                d_down_bias,
            ]
        )
        row_grad = lax.dynamic_update_slice_in_dim(row_grad, d_attn_bias, bias_start, 0)
        row_grad = lax.dynamic_update_slice_in_dim(row_grad, d_up_bias[:hidden_dev], up_start, 0)
        row_grad = lax.dynamic_update_slice_in_dim(
            row_grad, d_up_bias[hidden_dev:], other_up_start, 0
        )
        vector_rows[depth] = row_grad
    qkv_cols = 3 * heads_dev * HD
    pair_half = 2 * hidden_dev
    both_qkv = jnp.concatenate(held_qkv, axis=1).reshape(N_DP, BLOCK, LAYERS * qkv_cols)
    pieces = jnp.stack(vector_rows).reshape(N_MP, -1, 128)
    mine = jnp.sum(exchange(pieces), axis=0)
    high = lax.reduce_precision(mine, 8, 7)
    middle = lax.reduce_precision(mine - high, 8, 7)
    low = mine - high - middle
    split = jnp.stack([high, middle, low]).astype(bf16).reshape(-1, LAYERS * qkv_cols)
    split = jnp.broadcast_to(split[None], (N_DP,) + split.shape)
    pieces = exchange_dp(jnp.concatenate([both_qkv, split], axis=1)).astype(f32)
    both_qkv = jnp.sum(pieces[:, :BLOCK], axis=0)
    mine = jnp.sum(pieces[:, BLOCK:].reshape(N_DP, 3, -1, 128), axis=(0, 1))
    mine, held[0] = lax.optimization_barrier((mine, held[0]))
    from_other = pair_swap(
        jnp.concatenate([held[d][:, pair_half : 2 * pair_half] for d in range(LAYERS)], axis=1)
    )
    out_parts = jnp.stack([held[d][:, 2 * pair_half :] for d in range(LAYERS)])
    out_parts = out_parts.reshape(LAYERS * BLOCK, N_MP, 128)
    out_parts = jnp.transpose(out_parts, (1, 0, 2)).astype(f32)
    copies = jnp.broadcast_to(mine[None], (N_MP,) + mine.shape)
    pieces = exchange(jnp.concatenate([copies, out_parts], axis=1))
    vector_grad = pieces[:, : mine.shape[0]].reshape(LAYERS, -1)
    out_parts = jnp.sum(pieces[:, mine.shape[0] :], axis=0).reshape(LAYERS, BLOCK, 128)
    for depth in range(LAYERS):
        other = from_other[:, depth * pair_half : (depth + 1) * pair_half].astype(f32)
        g_mlp = held[depth][:, :pair_half].astype(f32) + other
        layer_grads[depth] = (
            both_qkv[:, depth * qkv_cols : (depth + 1) * qkv_cols],
            out_parts[depth].T,
            g_mlp[:, :hidden_dev],
            g_mlp[:, hidden_dev:].T,
        )
    owned = tuple(
        (jnp.stack([layer_grads[depth][kind] for depth in range(LAYERS)]) for kind in range(4))
    )
    out_tokens = (last_base + last_branch.astype(f32)).astype(bf16)
    out_rate = 0.8 / math.sqrt(D // 16)
    new_qkv, new_first_qkv, new_second_qkv = adam_step(
        w_qkv, first_qkv, second_qkv, owned[0], RATE_MATRIX, DECAY_MATRIX
    )
    new_out, new_first_out, new_second_out = adam_step(
        w_out, first_out, second_out, owned[1], out_rate, DECAY_MATRIX
    )
    new_up, new_first_up, new_second_up = adam_step(
        w_up, first_up, second_up, owned[2], RATE_MATRIX, DECAY_MATRIX
    )
    new_down, new_first_down, new_second_down = adam_step(
        w_down, first_down, second_down, owned[3], RATE_MATRIX, DECAY_MATRIX
    )
    new_vectors, new_vec_first, new_vec_second = adam_step(
        vectors, vec_first, vec_second, vector_grad, RATE_VECTOR, 0.0
    )
    bias_grads = jnp.stack(
        [vector_grad[:, 4 * D : 5 * D], vector_grad[:, 7 * D + FF : 8 * D + FF]], axis=1
    )
    return (
        out_tokens,
        grad_flow,
        new_qkv,
        new_out,
        new_up,
        new_down,
        new_first_qkv,
        new_first_out,
        new_first_up,
        new_first_down,
        new_second_qkv,
        new_second_out,
        new_second_up,
        new_second_down,
        new_vectors,
        new_vec_first,
        new_vec_second,
        bias_grads,
    )


def solution(mesh):
    placed = (
        P(("dp", "mp"), None),
        P(("dp", "mp"), None),
        P("dp", None),
        P(None, "dp", "mp"),
        P(None, "mp", "dp"),
        P(None, "dp", "mp"),
        P(None, "mp", "dp"),
        P(None, "dp", "mp"),
        P(None, "mp", "dp"),
        P(None, "dp", "mp"),
        P(None, "mp", "dp"),
        P(None, "dp", "mp"),
        P(None, "mp", "dp"),
        P(None, "dp", "mp"),
        P(None, "mp", "dp"),
        P(),
        P(),
        P(),
    )
    return jax.shard_map(
        local,
        mesh=mesh,
        in_specs=placed,
        out_specs=(
            P(("dp", "mp"), None),
            P(("dp", "mp"), None),
            P(None, "dp", "mp"),
            P(None, "mp", "dp"),
            P(None, "dp", "mp"),
            P(None, "mp", "dp"),
            P(None, "dp", "mp"),
            P(None, "mp", "dp"),
            P(None, "dp", "mp"),
            P(None, "mp", "dp"),
            P(None, "dp", "mp"),
            P(None, "mp", "dp"),
            P(None, "dp", "mp"),
            P(None, "mp", "dp"),
            P(),
            P(),
            P(),
            P(),
        ),
        check_vma=False,
    )
```

time: 1800 us -> 543 us (0.30)
  waiting for transfers between devices: 1440 us -> 203 us
  starting transfers between devices: 2.17 us -> 66.2 us
  matrix products: 113 us -> 56 us
  Pallas kernels: 0 us -> 26.8 us
  blocking collectives: 116 us -> 89.6 us
  other arithmetic: 54.9 us -> 36.6 us
    reduce_scatter x16 -> x3, waiting for transfers between devices: 922 us -> 17.4 us  [the longest x2 17.3 us: scatter_dp(): return lax.psum_scatter(values, DP, scatter_dimension=0, tiled=True)]
    all_gather x12 -> x3, waiting for transfers between devices: 378 us -> 9.96 us  [the longest x1 7.48 us: local(): lax.all_gather(cotangent, MP, axis=0, tiled=True, axis_index_groups=COLUMNS)]
    all_to_all x0 -> x13, waiting for transfers between devices: none -> 170 us  [the longest x8 88.3 us: exchange(): return lax.all_to_all(pieces, MP, 0, 0)]
    psum x1 -> x0, waiting for transfers between devices: 135 us -> none  [local(): vector_grad = lax.psum(jnp.stack(vector_rows), ('dp', 'mp'))]
    all_gather x4 -> x0, blocking collectives: 116 us -> none  [the longest x2 60.8 us: local(): lax.all_gather(fetch_rounded_qkv, 'dp', axis=0, tiled=True)]
    all_to_all x0 -> x6, blocking collectives: none -> 89.6 us  [the longest x3 48.1 us: exchange(): return lax.all_to_all(pieces, MP, 0, 0)]
    all_to_all x0 -> x13, starting transfers between devices: none -> 63.2 us  [the longest x8 36.6 us: exchange(): return lax.all_to_all(pieces, MP, 0, 0)]
    dot_general x34 -> x8, matrix products: 52.9 us -> 23.3 us  [the longest x2 9.32 us: local(): jnp.dot(normed_two, weights[:, :CUT_DOWN], preferred_element_type=f32)]
  transfers between devices with their start and end apart: 29 -> 21, of which waited for: 27 -> 15; matrix products, arithmetic and copies ran while one was open for 5% -> 17% of each run, Pallas kernels for 0% -> 4%
where the time goes in v1:
time: 543 us; the launch traced here: 533 us
  waiting for transfers between devices  203 us (37%)
  blocking collectives  89.6 us (17%)
  starting transfers between devices  66.2 us (12%)
  matrix products  56 us (10%)
  local copies, waits for them, and re-layouts  36.7 us (7%)
  other arithmetic  36.6 us (7%)
  Pallas kernels  26.8 us (5%)
  between operations  17.4 us (3%)
    all_to_all x8, waiting for transfers between devices, exchange(): return lax.all_to_all(pieces, MP, 0, 0)  88.3 us
    all_to_all x3, blocking collectives, exchange(): return lax.all_to_all(pieces, MP, 0, 0)  48.1 us
    all_to_all x2, waiting for transfers between devices, exchange_dp(): return lax.all_to_all(pieces, DP, 0, 0)  45.5 us
    all_to_all x3, blocking collectives, exchange_column(): return lax.all_to_all(pieces, MP, 0, 0, axis_index_groups=COLUMNS)  41.5 us
    all_to_all x8, starting transfers between devices, exchange(): return lax.all_to_all(pieces, MP, 0, 0)  36.6 us
    all_to_all x3, waiting for transfers between devices, exchange_column(): return lax.all_to_all(pieces, MP, 0, 0, axis_index_groups=COLUMNS)  36 us
    unnamed x189, local copies, waits for them, and re-layouts  20.5 us
    dot_general x6, matrix products, contract_cols(): lax.dot_general(left, right, (((1,), (1,)), ((), ())), preferred_element_...  19.5 us
  transfers between devices with their start and end apart: 21, of which 15 were waited for; matrix products, arithmetic and copies ran while one was open for 17% of the time, Pallas kernels for 4%

profile of v1, /device:TPU:0, one launch (start us, length us, event | category | flops | bytes accessed | tf_op | source)
XLA Modules:
  0.0 532.5 jit_solution(13234716593427998264)
XLA Ops:
  12.8 5.3 %collective-permute-done = bf16[64,2048]{1,0:T(8,128)(2,1)S(1)} collective-permute-done((bf16[64,2048]{1,0:T(8,128)(2,1)S(1)}, bf16[64,2048]{1,0:T(8,128)(2,1)S(1)}, u32[]{:S(2)}, u32[]{:S(2)}) %collective-permute-start) | collective-permute-done | bytes 262176 | tf_op jit(solution)/shard_map/ppermute | solution.py:89
  19.7 5.6 %all-to-all-start.2 = ((bf16[8,2,128,64]{2,3,1,0:T(8,128)(2,1)}), bf16[8,2,128,64]{2,3,1,0:T(8,128)(2,1)S(1)}, u32[]{:S(2)}, u32[]{:S(2)}) async-start(bf16[8,2,128,64]{2,3,1,0:T(8,128)(2,1)} %broadcast_in_dim.32), calls=%async_computation.2 | async-start | bytes 524288 | tf_op jit(solution)/shard_map/all_to_all | solution.py:93
  25.8 6.9 %all-to-all-done.2 = bf16[8,2,128,64]{2,3,1,0:T(8,128)(2,1)S(1)} async-done(((bf16[8,2,128,64]{2,3,1,0:T(8,128)(2,1)}), bf16[8,2,128,64]{2,3,1,0:T(8,128)(2,1)S(1)}, u32[]{:S(2)}, u32[]{:S(2)}) %all-to-all-start.2) | async-done | bytes 262176 | tf_op jit(solution)/shard_map/all_to_all | solution.py:93
  39.1 33.5 %all-to-all-done = bf16[8,128,1024]{2,1,0:T(8,128)(2,1)S(1)} async-done(((bf16[8,128,1024]{2,1,0:T(8,128)(2,1)}), bf16[8,128,1024]{2,1,0:T(8,128)(2,1)S(1)}, u32[]{:S(2)}, u32[]{:S(2)}) %all-to-all-start) | async-done | bytes 2097184 | tf_op jit(solution)/shard_map/all_to_all | solution.py:93
  74.8 8.7 %all-to-all-start.3 = ((bf16[16,64,1024]{2,1,0:T(8,128)(2,1)}), bf16[16,64,1024]{2,1,0:T(8,128)(2,1)S(1)}, u32[]{:S(2)}, u32[]{:S(2)}) async-start(bf16[16,64,1024]{2,1,0:T(8,128)(2,1)} %broadcast_in_dim.34), calls=%async_computation.3 | async-start | bytes 4194304 | tf_op jit(solution)/shard_map/all_to_all | solution.py:121
  94.6 22.8 %all-to-all-done.3 = bf16[16,64,1024]{2,1,0:T(8,128)(2,1)S(1)} async-done(((bf16[16,64,1024]{2,1,0:T(8,128)(2,1)}), bf16[16,64,1024]{2,1,0:T(8,128)(2,1)S(1)}, u32[]{:S(2)}, u32[]{:S(2)}) %all-to-all-start.3) | async-done | bytes 2097184 | tf_op jit(solution)/shard_map/all_to_all | solution.py:121
  117.3 9.7 %all_to_all.95 = bf16[8,128,128]{2,1,0:T(8,128)(2,1)S(1)} all-to-all(bf16[8,128,128]{2,1,0:T(8,128)(2,1)S(1)} %get-tuple-element.37), channel_id=1, replica_groups=mesh['dp'=16,'mp'=8] {'mp'}, dimensions={0} | all-to-all | bytes 524288 | tf_op jit(solution)/shard_map/all_to_all | solution.py:93
  133.0 12.9 %all-to-all-done.4 = bf16[4,128,1024]{2,1,0:T(8,128)(2,1)S(1)} async-done(((bf16[4,128,1024]{2,1,0:T(8,128)(2,1)}), bf16[4,128,1024]{2,1,0:T(8,128)(2,1)S(1)}, u32[]{:S(2)}, u32[]{:S(2)}) %all-to-all-start.4) | async-done | bytes 1048608 | tf_op jit(solution)/shard_map/all_to_all | solution.py:97
  154.1 14.4 %all_to_all.96 = bf16[4,128,1024]{2,1,0:T(8,128)(2,1)S(1)} all-to-all(bf16[4,128,1024]{2,1,0:T(8,128)(2,1)S(1)} %bitcast.203), channel_id=1, replica_groups={{0,2,4,6},{1,3,5,7},{8,10,12,14},{9,11,13,15},{16,18,20,22},{17,19,21,2..., dimensions={0} | all-to-all | bytes 2097152 | tf_op jit(solution)/shard_map/all_to_all | solution.py:97
  175.5 22.6 %all-to-all-done.6 = bf16[8,128,1024]{2,1,0:T(8,128)(2,1)} async-done(((bf16[8,128,1024]{2,1,0:T(8,128)(2,1)}), bf16[8,128,1024]{2,1,0:T(8,128)(2,1)}, u32[]{:S(2)}, u32[]{:S(2)}) %all-to-all-start.6) | async-done | bytes 2097184 | tf_op jit(solution)/shard_map/all_to_all | solution.py:93
  204.9 9.8 %all_to_all.97 = bf16[8,128,128]{2,1,0:T(8,128)(2,1)S(1)} all-to-all(bf16[8,128,128]{2,1,0:T(8,128)(2,1)S(1)} %get-tuple-element.38), channel_id=1, replica_groups=mesh['dp'=16,'mp'=8] {'mp'}, dimensions={0} | all-to-all | bytes 524288 | tf_op jit(solution)/shard_map/all_to_all | solution.py:93
  223.6 10.3 %all-to-all-done.8 = bf16[4,128,1024]{2,1,0:T(8,128)(2,1)S(1)} async-done(((bf16[4,128,1024]{2,1,0:T(8,128)(2,1)}), bf16[4,128,1024]{2,1,0:T(8,128)(2,1)S(1)}, u32[]{:S(2)}, u32[]{:S(2)}) %all-to-all-start.8) | async-done | bytes 1048608 | tf_op jit(solution)/shard_map/all_to_all | solution.py:97
  242.8 7.5 %all-gather.8.cloned.1.call-done.d_mlp_ref = bf16[512,1024]{1,0:T(8,128)(2,1)} async-done(((bf16[128,1024]{1,0:T(8,128)(2,1)}), bf16[512,1024]{1,0:T(8,128)(2,1)}) %all-gather.8.cloned.1.call-update) | async-done | bytes 1048592 | tf_op jit(solution)/shard_map/all_gather | solution.py:445
  263.9 12.8 %all-to-all-done.9 = bf16[4,128,1024]{2,1,0:T(8,128)(2,1)} async-done(((bf16[4,128,1024]{2,1,0:T(8,128)(2,1)}), bf16[4,128,1024]{2,1,0:T(8,128)(2,1)}, u32[]{:S(2)}, u32[]{:S(2)}) %all-to-all-start.9) | async-done | bytes 1048608 | tf_op jit(solution)/shard_map/all_to_all | solution.py:97
  300.2 6.7 %shard_map.316 = (bf16[1024,384]{1,0:T(8,128)(2,1)S(1)}, f32[1,384]{1,0:T(1,128)S(1)}) custom-call(f32[2]{0:T(128)S(1)} %multiply_exponential_fusion.slopes_ref, bf16[1024,384]{1,0:T(8,128)(2,1)S(1)} %copy-done.18, bf16[1024,128]{1,0:T(8,128)(2,1)} %bitcast.42.d_context_ref, f32[1,1024]{1,0:T(1,128)S(1)} %bitcast.190, f32[2,1024]{1,0:T(2,128)S(1)} %get-tuple-element.41.log_ref), custom_call_target="tpu_custom_call" | custom-call | flops 2684354560 | bytes 2097152 | tf_op jit(solution)/shard_map/pallas_call | solution.py:293
  309.7 28.7 %all_to_all.98 = bf16[8,128,1024]{2,1,0:T(8,128)(2,1)S(1)} all-to-all(bf16[8,128,1024]{2,1,0:T(8,128)(2,1)S(1)} %bitcast.198), channel_id=1, replica_groups=mesh['dp'=16,'mp'=8] {'mp'}, dimensions={0} | all-to-all | bytes 4194304 | tf_op jit(solution)/shard_map/all_to_all | solution.py:93
  341.0 13.6 %all_to_all.99 = bf16[4,128,1024]{2,1,0:T(8,128)(2,1)S(1)} all-to-all(bf16[4,128,1024]{2,1,0:T(8,128)(2,1)S(1)} %broadcast_in_dim.38), channel_id=1, replica_groups={{0,2,4,6},{1,3,5,7},{8,10,12,14},{9,11,13,15},{16,18,20,22},{17,19,21,2..., dimensions={0} | all-to-all | bytes 2097152 | tf_op jit(solution)/shard_map/all_to_all | solution.py:97
  359.0 13.4 %all_to_all.100 = bf16[4,128,1024]{2,1,0:T(8,128)(2,1)S(1)} all-to-all(bf16[4,128,1024]{2,1,0:T(8,128)(2,1)S(1)} %bitcast.204), channel_id=1, replica_groups={{0,2,4,6},{1,3,5,7},{8,10,12,14},{9,11,13,15},{16,18,20,22},{17,19,21,2..., dimensions={0} | all-to-all | bytes 2097152 | tf_op jit(solution)/shard_map/all_to_all | solution.py:97
  395.1 6.7 %shard_map.318 = (bf16[1024,384]{1,0:T(8,128)(2,1)S(1)}, f32[1,384]{1,0:T(1,128)S(1)}) custom-call(f32[2]{0:T(128)S(1)} %multiply_exponential_fusion.slopes_ref, bf16[1024,384]{1,0:T(8,128)(2,1)S(1)} %copy-done.16, bf16[1024,128]{1,0:T(8,128)(2,1)} %bitcast.47.d_context_ref, f32[1,1024]{1,0:T(1,128)S(1)} %bitcast.191, f32[2,1024]{1,0:T(2,128)S(1)} %get-tuple-element.44.log_ref), custom_call_target="tpu_custom_call" | custom-call | flops 2684354560 | bytes 2097152 | tf_op jit(solution)/shard_map/pallas_call | solution.py:293
  405.7 6.0 %all-to-all-start.15 = ((bf16[8,128,1024]{2,1,0:T(8,128)(2,1)}), bf16[8,128,1024]{2,1,0:T(8,128)(2,1)S(1)}, u32[]{:S(2)}, u32[]{:S(2)}) async-start(bf16[8,128,1024]{2,1,0:T(8,128)(2,1)} %bitcast.197), calls=%async_computation.17 | async-start | bytes 4194304 | tf_op jit(solution)/shard_map/all_to_all | solution.py:93
  415.8 15.9 %all-to-all-done.15 = bf16[8,128,1024]{2,1,0:T(8,128)(2,1)S(1)} async-done(((bf16[8,128,1024]{2,1,0:T(8,128)(2,1)}), bf16[8,128,1024]{2,1,0:T(8,128)(2,1)S(1)}, u32[]{:S(2)}, u32[]{:S(2)}) %all-to-all-start.15) | async-done | bytes 2097184 | tf_op jit(solution)/shard_map/all_to_all | solution.py:93
  447.7 6.6 %all-to-all-start.17 = ((bf16[16,76,768]{2,1,0:T(8,128)(2,1)}), bf16[16,76,768]{2,1,0:T(8,128)(2,1)S(1)}, u32[]{:S(2)}, u32[]{:S(2)}) async-start(bf16[16,76,768]{2,1,0:T(8,128)(2,1)} %pad_maximum_fusion), calls=%async_computation.19 | async-start | bytes 3932160 | tf_op jit(solution)/shard_map/all_to_all | solution.py:121
  459.8 22.8 %all-to-all-done.17 = bf16[16,76,768]{2,1,0:T(8,128)(2,1)S(1)} async-done(((bf16[16,76,768]{2,1,0:T(8,128)(2,1)}), bf16[16,76,768]{2,1,0:T(8,128)(2,1)S(1)}, u32[]{:S(2)}, u32[]{:S(2)}) %all-to-all-start.17) | async-done | bytes 1867808 | tf_op jit(solution)/shard_map/all_to_all | solution.py:121
  487.2 17.3 %reduce-scatter.8.cloned.1.call-done = bf16[64,3072]{1,0:T(8,128)(2,1)} async-done(((bf16[1024,3072]{1,0:T(8,128)(2,1)}), bf16[64,3072]{1,0:T(8,128)(2,1)}) %reduce-scatter.8.cloned.1.call-update) | async-done | bytes 393232 | tf_op jit(solution)/shard_map/reduce_scatter | solution.py:134
  (379 shorter events, 194.5 us)
Async XLA Ops:
  8.0 78.8 %all-gather.4.cloned.1.call-start = ((), (), s32[]{:S(2)}) async-start(), calls=%async_computation.22 | async-start | bytes 5292032 | tf_op jit(solution)/shard_map/all_gather | solution.py:130
  10.1 8.0 %collective-permute-start = (bf16[64,2048]{1,0:T(8,128)(2,1)S(1)}, bf16[64,2048]{1,0:T(8,128)(2,1)S(1)}, u32[]{:S(2)}, u32[]{:S(2)}) collective-permute-start(bf16[64,2048]{1,0:T(8,128)(2,1)S(1)} %pad_maximum_fusion.3), channel_id=1, source_target_pairs={{0,1},{1,0},{2,3},{3,2},{4,5},{5,4},{6,7},{7,6},{8,9},{9,8},{10,11... | collective-permute-start | bytes 786440 | tf_op jit(solution)/shard_map/ppermute | solution.py:89
  19.7 12.9 %all-to-all-start.2 = ((bf16[8,2,128,64]{2,3,1,0:T(8,128)(2,1)}), bf16[8,2,128,64]{2,3,1,0:T(8,128)(2,1)S(1)}, u32[]{:S(2)}, u32[]{:S(2)}) async-start(bf16[8,2,128,64]{2,3,1,0:T(8,128)(2,1)} %broadcast_in_dim.32), calls=%async_computation.2 | async-start | bytes 524288 | tf_op jit(solution)/shard_map/all_to_all | solution.py:93
  25.4 172.7 %all-gather.6.cloned.1.call-start = ((), (), s32[]{:S(2)}) async-start(), calls=%async_computation.23 | async-start | bytes 7520256 | tf_op jit(solution)/shard_map/all_gather | solution.py:130
  35.5 37.2 %all-to-all-start = ((bf16[8,128,1024]{2,1,0:T(8,128)(2,1)}), bf16[8,128,1024]{2,1,0:T(8,128)(2,1)S(1)}, u32[]{:S(2)}, u32[]{:S(2)}) async-start(bf16[8,128,1024]{2,1,0:T(8,128)(2,1)} %broadcast_in_dim.30), calls=%async_computation | async-start | bytes 4194304 | tf_op jit(solution)/shard_map/all_to_all | solution.py:93
  74.8 42.6 %all-to-all-start.3 = ((bf16[16,64,1024]{2,1,0:T(8,128)(2,1)}), bf16[16,64,1024]{2,1,0:T(8,128)(2,1)S(1)}, u32[]{:S(2)}, u32[]{:S(2)}) async-start(bf16[16,64,1024]{2,1,0:T(8,128)(2,1)} %broadcast_in_dim.34), calls=%async_computation.3 | async-start | bytes 4194304 | tf_op jit(solution)/shard_map/all_to_all | solution.py:121
  129.5 16.5 %all-to-all-start.4 = ((bf16[4,128,1024]{2,1,0:T(8,128)(2,1)}), bf16[4,128,1024]{2,1,0:T(8,128)(2,1)S(1)}, u32[]{:S(2)}, u32[]{:S(2)}) async-start(bf16[4,128,1024]{2,1,0:T(8,128)(2,1)} %broadcast_in_dim.35), calls=%async_computation.4 | async-start | bytes 2097152 | tf_op jit(solution)/shard_map/all_to_all | solution.py:97
  170.9 27.2 %all-to-all-start.6 = ((bf16[8,128,1024]{2,1,0:T(8,128)(2,1)}), bf16[8,128,1024]{2,1,0:T(8,128)(2,1)}, u32[]{:S(2)}, u32[]{:S(2)}) async-start(bf16[8,128,1024]{2,1,0:T(8,128)(2,1)} %broadcast_in_dim.36), calls=%async_computation.6 | async-start | bytes 4194304 | tf_op jit(solution)/shard_map/all_to_all | solution.py:93
  217.3 61.1 %copy-start.64 = (f32[128]{0:T(128)}, f32[128]{0:T(128)S(1)}, u32[]{:S(2)}) copy-start(f32[128]{0:T(128)S(1)} %broadcast_multiply_fusion.8) | copy-start | bytes 1540
  217.5 60.9 %copy-start.69 = (f32[128]{0:T(128)}, f32[128]{0:T(128)S(1)}, u32[]{:S(2)}) copy-start(f32[128]{0:T(128)S(1)} %add_rsqrt_fusion) | copy-start | bytes 1540
  219.5 14.4 %all-to-all-start.8 = ((bf16[4,128,1024]{2,1,0:T(8,128)(2,1)}), bf16[4,128,1024]{2,1,0:T(8,128)(2,1)S(1)}, u32[]{:S(2)}, u32[]{:S(2)}) async-start(bf16[4,128,1024]{2,1,0:T(8,128)(2,1)} %broadcast_in_dim.37), calls=%async_computation.8 | async-start | bytes 2097152 | tf_op jit(solution)/shard_map/all_to_all | solution.py:97
  223.0 27.3 %all-gather.8.cloned.1.call-start = ((), (), s32[]{:S(2)}) async-start(), calls=%async_computation.24 | async-start | bytes 1310720 | tf_op jit(solution)/shard_map/all_gather | solution.py:445
  259.1 17.6 %all-to-all-start.9 = ((bf16[4,128,1024]{2,1,0:T(8,128)(2,1)}), bf16[4,128,1024]{2,1,0:T(8,128)(2,1)}, u32[]{:S(2)}, u32[]{:S(2)}) async-start(bf16[4,128,1024]{2,1,0:T(8,128)(2,1)} %bitcast.202), calls=%async_computation.9 | async-start | bytes 2097152 | tf_op jit(solution)/shard_map/all_to_all | solution.py:97
  263.4 138.4 %reduce-scatter.6.cloned.1.call-start = ((), (), s32[]{:S(2)}) async-start(), calls=%async_computation.26 | async-start | bytes 1310720 | tf_op jit(solution)/shard_map/reduce_scatter | solution.py:520
  285.9 13.2 %all-to-all-start.10 = ((bf16[8,128,128]{2,1,0:T(8,128)(2,1)}), bf16[8,128,128]{2,1,0:T(8,128)(2,1)}, u32[]{:S(2)}, u32[]{:S(2)}) async-start(bf16[8,128,128]{2,1,0:T(8,128)(2,1)} %bitcast.206), calls=%async_computation.10 | async-start | bytes 524288 | tf_op jit(solution)/shard_map/all_to_all | solution.py:93
  289.9 111.9 %reduce-scatter.4.cloned.1.call-start = ((), (), s32[]{:S(2)}) async-start(), calls=%async_computation.25 | async-start | bytes 6684672 | tf_op jit(solution)/shard_map/reduce_scatter | solution.py:134
  306.9 47.7 %slice-start = ((s8[4980736]{0:T(1024)(128)(4,1)}), s8[786432]{0:T(1024)(128)(4,1)S(1)}, s32[]{:S(2)}) async-start(s8[4980736]{0:T(1024)(128)(4,1)} %bitcast.238), calls=%async_computation.28 | async-start | bytes 1572864
  377.1 13.3 %all-to-all-start.14 = ((bf16[8,128,128]{2,1,0:T(8,128)(2,1)}), bf16[8,128,128]{2,1,0:T(8,128)(2,1)}, u32[]{:S(2)}, u32[]{:S(2)}) async-start(bf16[8,128,128]{2,1,0:T(8,128)(2,1)} %bitcast.205), calls=%async_computation.14 | async-start | bytes 524288 | tf_op jit(solution)/shard_map/all_to_all | solution.py:93
  381.1 123.4 %reduce-scatter.8.cloned.1.call-start = ((), (), s32[]{:S(2)}) async-start(), calls=%async_computation.27 | async-start | bytes 6684672 | tf_op jit(solution)/shard_map/reduce_scatter | solution.py:134
  405.7 26.1 %all-to-all-start.15 = ((bf16[8,128,1024]{2,1,0:T(8,128)(2,1)}), bf16[8,128,1024]{2,1,0:T(8,128)(2,1)S(1)}, u32[]{:S(2)}, u32[]{:S(2)}) async-start(bf16[8,128,1024]{2,1,0:T(8,128)(2,1)} %bitcast.197), calls=%async_computation.17 | async-start | bytes 4194304 | tf_op jit(solution)/shard_map/all_to_all | solution.py:93
  433.9 10.7 %all-to-all-start.16 = ((f32[8,24,128]{2,1,0:T(8,128)}), f32[8,24,128]{2,1,0:T(8,128)S(1)}, u32[]{:S(2)}, u32[]{:S(2)}) async-start(f32[8,24,128]{2,1,0:T(8,128)} %reshape.350), calls=%async_computation.18 | async-start | bytes 196608 | tf_op jit(solution)/shard_map/all_to_all | solution.py:93
  447.7 34.9 %all-to-all-start.17 = ((bf16[16,76,768]{2,1,0:T(8,128)(2,1)}), bf16[16,76,768]{2,1,0:T(8,128)(2,1)S(1)}, u32[]{:S(2)}, u32[]{:S(2)}) async-start(bf16[16,76,768]{2,1,0:T(8,128)(2,1)} %pad_maximum_fusion), calls=%async_computation.19 | async-start | bytes 3932160 | tf_op jit(solution)/shard_map/all_to_all | solution.py:121
  505.5 8.1 %collective-permute-start.1 = (bf16[64,2048]{1,0:T(8,128)(2,1)S(1)}, bf16[64,2048]{1,0:T(8,128)(2,1)}, u32[]{:S(2)}, u32[]{:S(2)}) collective-permute-start(bf16[64,2048]{1,0:T(8,128)(2,1)S(1)} %pad_maximum_fusion.4), channel_id=1, source_target_pairs={{0,1},{1,0},{2,3},{3,2},{4,5},{5,4},{6,7},{7,6},{8,9},{9,8},{10,11... | collective-permute-start | bytes 786440 | tf_op jit(solution)/shard_map/ppermute | solution.py:89
  507.4 14.8 %all-to-all-start.18 = ((f32[8,152,128]{2,1,0:T(8,128)}), f32[8,152,128]{2,1,0:T(8,128)S(1)}, u32[]{:S(2)}, u32[]{:S(2)}) async-start(f32[8,152,128]{2,1,0:T(8,128)} %pad_maximum_fusion.2), calls=%async_computation.21 | async-start | bytes 1245184 | tf_op jit(solution)/shard_map/all_to_all | solution.py:93
  (81 other events, 641.6 us)
Sparse Core Ops, SparseCore 0:
  19.0 67.6 all-gather.3
  89.8 71.5 all-gather.5
Sparse Core Ops, SparseCore 1:
  225.1 25.1 all-gather.7
  266.2 25.6 reduce-scatter.5
  299.2 92.7 reduce-scatter.3
  396.1 108.3 reduce-scatter.7
